TPU v7x, 32 devices: a whole 2x2x4 slice. The times are simulated.
32 devices in a mesh: ctx: 8 (over z, y), wa: 4 (over x, core).
Axes of the slice: x: 2, y: 2, z: 4, core: 2. Of those that a mesh axis runs over, the one named last changes fastest.
Arguments:
- tokens: bfloat16 [6144, 576], P(('ctx', 'wa')), may hold values from -6 to 6
- segment_ids: int32 [6144], replicated, may hold values from 0 to 5, as said below
- w_query: bfloat16 [576, 576], P('wa'), may hold values from -0.5 to 0.5
- w_key: bfloat16 [576, 192], P('wa'), may hold values from -0.25 to 0.25
- w_value: bfloat16 [576, 192], P('wa'), may hold values from -0.25 to 0.25
- w_out: bfloat16 [576, 576], P('wa'), may hold values from -1.5 to 1.5
- w_gate: bfloat16 [576, 1536], P('wa'), may hold values from -0.25 to 0.25
- w_up: bfloat16 [576, 1536], P('wa'), may hold values from -0.25 to 0.25
- w_down: bfloat16 [1536, 576], P('wa'), may hold values from -0.15625 to 0.15625
- gain_attn: bfloat16 [576], P('wa'), may hold values from 0.5 to 1.5
- gain_ffn: bfloat16 [576], P('wa'), may hold values from 0.5 to 1.5
- cotangent: bfloat16 [6144, 576], P(('ctx', 'wa')), may hold values from -6 to 6
Outputs:
- output: bfloat16 [6144, 576], P(('ctx', 'wa'))
- grad_tokens: bfloat16 [6144, 576], P(('ctx', 'wa'))
- grad_query: float32 [576, 576], P('wa')
- grad_key: float32 [576, 192], P('wa')
- grad_value: float32 [576, 192], P('wa')
- grad_out: float32 [576, 576], P('wa')
- grad_gate: float32 [576, 1536], P('wa')
- grad_up: float32 [576, 1536], P('wa')
- grad_down: float32 [1536, 576], P('wa')
- grad_gain_attn: float32 [576], P('wa')
- grad_gain_ffn: float32 [576], P('wa')
Inputs may be any that keep to these rules, and one draw needn't show every extreme that they name: `segment_ids`: ids never decrease along the tokens, and no document (the tokens of one id) has tokens on both sides of position 3072.
All inputs are finite; a program needn't handle non-finite values.
Results may differ from a plain program's by a relative error of at most 0.02.
Values may be sent and summed in bfloat16 or wider, within the bound.
A program may use at most 64 MiB of HBM per device.

v0:
```python
import jax
import jax.numpy as jnp
from jax import lax
from jax.sharding import PartitionSpec as P

HEADS = 9
KV_HEADS = 3
HEAD_DIM = 64


EPSILON = 1e-05
ROPE_BASE = 100000.0
MASKED_SCORE = -1e30


def passed_along(shard, axis, by):
    count = lax.axis_size(axis)
    pairs = [(i, i + by) for i in range(count) if 0 <= i + by < count]
    return lax.ppermute(shard, axis, pairs)


def shifted(block, axis, distance):
    devices = range(lax.axis_size(axis))
    route = [((i - distance) % len(devices), i) for i in devices]
    return lax.ppermute(block, axis, route)


def rms_scale(vector):
    return lax.rsqrt(jnp.mean(vector * vector, axis=-1, keepdims=True) + EPSILON)


def rotate(tensor, cosine_table, sine_table):
    half_dim = tensor.shape[-1] // 2
    front_part = tensor[..., :half_dim]
    back_part = tensor[..., half_dim:]
    return jnp.concatenate(
        [
            front_part * cosine_table - back_part * sine_table,
            back_part * cosine_table + front_part * sine_table,
        ],
        axis=-1,
    )


def unrotate(gradient, cosine_table, sine_table):
    half_dim = gradient.shape[-1] // 2
    front_part = gradient[..., :half_dim]
    back_part = gradient[..., half_dim:]
    return jnp.concatenate(
        [
            front_part * cosine_table + back_part * sine_table,
            back_part * cosine_table - front_part * sine_table,
        ],
        axis=-1,
    )


def rope_tables(positions, head_size):
    half_dim = head_size // 2
    frequency = ROPE_BASE ** (-(jnp.arange(half_dim, dtype=jnp.float32) * 2.0) / head_size)
    angle_table = positions.astype(jnp.float32)[:, None] * frequency[None, :]
    return (jnp.cos(angle_table)[:, None, :], jnp.sin(angle_table)[:, None, :])


def norm_back(gradient, vector, row_scale, gain_row):
    gain_grad = jnp.sum(gradient * (vector * row_scale), axis=0)
    scaled = gradient * gain_row
    input_grad = row_scale * scaled - row_scale * row_scale * row_scale * vector * jnp.mean(
        scaled * vector, axis=-1, keepdims=True
    )
    return (input_grad, gain_grad)


def on_device(
    tokens,
    segment_ids,
    w_query,
    w_key,
    w_value,
    w_out,
    w_gate,
    w_up,
    w_down,
    gain_attn,
    gain_ffn,
    cotangent,
):
    row_count = tokens.shape[0]
    ctx_count = lax.axis_size("ctx")
    wa_count = lax.axis_size("wa")
    ctx_index = lax.axis_index("ctx")
    wa_index = lax.axis_index("wa")
    block_rows = row_count * wa_count
    half_blocks = ctx_count // 2
    group_size = HEADS // KV_HEADS
    kv_width = KV_HEADS * HEAD_DIM
    score_scale = HEAD_DIM ** (-0.5)
    row_start = (ctx_index * wa_count + wa_index) * row_count
    gathered = (
        lax.all_gather(w_query, "wa", axis=0, tiled=True),
        lax.all_gather(w_key, "wa", axis=0, tiled=True),
        lax.all_gather(w_value, "wa", axis=0, tiled=True),
        lax.all_gather(w_out, "wa", axis=0, tiled=True),
        lax.all_gather(w_gate, "wa", axis=0, tiled=True),
        lax.all_gather(w_up, "wa", axis=0, tiled=True),
        lax.all_gather(w_down, "wa", axis=0, tiled=True),
        lax.all_gather(gain_attn, "wa", axis=0, tiled=True),
        lax.all_gather(gain_ffn, "wa", axis=0, tiled=True),
    )
    (
        query_full,
        key_full,
        value_full,
        out_full,
        gate_full,
        up_full,
        down_full,
        gain_one,
        gain_two,
    ) = gathered
    query_ids = row_start + jnp.arange(row_count, dtype=jnp.int32)
    query_segs = lax.dynamic_slice_in_dim(segment_ids, row_start, row_count)
    positions = query_ids - jnp.searchsorted(segment_ids, query_segs, side="left")
    cosine_table, sine_table = rope_tables(positions, HEAD_DIM)
    inputs = tokens.astype(jnp.float32)
    scale_one = rms_scale(inputs)
    gain_first = gain_one.astype(jnp.float32)
    normed = (inputs * scale_one * gain_first).astype(jnp.bfloat16)
    query_pre = jnp.dot(normed, query_full, preferred_element_type=jnp.float32).reshape(
        row_count, HEADS, HEAD_DIM
    )
    key_pre = jnp.dot(normed, key_full, preferred_element_type=jnp.float32).reshape(
        row_count, KV_HEADS, HEAD_DIM
    )
    value_low = jnp.dot(normed, value_full, preferred_element_type=jnp.float32).astype(jnp.bfloat16)
    query_low = rotate(query_pre, cosine_table, sine_table).astype(jnp.bfloat16)
    key_low = (
        rotate(key_pre, cosine_table, sine_table).astype(jnp.bfloat16).reshape(row_count, kv_width)
    )
    query_grid = query_low.reshape(row_count, KV_HEADS, group_size, HEAD_DIM).transpose(1, 2, 0, 3)
    own_block = lax.all_gather(
        jnp.concatenate([key_low, value_low], axis=1), "wa", axis=0, tiled=True
    )
    own_start = ctx_index * block_rows

    def block_start(offset):
        return jnp.mod(ctx_index - offset, ctx_count) * block_rows

    def scores_of(kv_block, key_start):
        key_rows = kv_block[:, :kv_width].reshape(block_rows, KV_HEADS, HEAD_DIM)
        value_rows = kv_block[:, kv_width:].reshape(block_rows, KV_HEADS, HEAD_DIM)
        raw_scores = (
            jnp.einsum("gird,kgd->girk", query_grid, key_rows, preferred_element_type=jnp.float32)
            * score_scale
        )
        key_ids = key_start + jnp.arange(block_rows, dtype=jnp.int32)
        key_segs = lax.dynamic_slice_in_dim(segment_ids, key_start, block_rows)
        allowed_pairs = (query_segs[:, None] == key_segs[None, :]) & (
            key_ids[None, :] <= query_ids[:, None]
        )
        return (jnp.where(allowed_pairs, raw_scores, MASKED_SCORE), key_rows, value_rows)

    def attend_block(running, kv_block, key_start):
        maxima, totals, summed = running
        masked, key_rows, value_rows = scores_of(kv_block, key_start)
        new_max = jnp.maximum(maxima, jnp.max(masked, axis=-1))
        factor = jnp.exp(maxima - new_max)
        exponent = jnp.exp(masked - new_max[..., None])
        totals = totals * factor + jnp.sum(exponent, axis=-1)
        summed = summed * factor[..., None] + jnp.einsum(
            "girk,kgd->gird",
            exponent.astype(jnp.bfloat16),
            value_rows,
            preferred_element_type=jnp.float32,
        )
        return (new_max, totals, summed)

    empty_max = jnp.full((KV_HEADS, group_size, row_count), MASKED_SCORE, jnp.float32)
    running = (
        empty_max,
        jnp.zeros((KV_HEADS, group_size, row_count), jnp.float32),
        jnp.zeros((KV_HEADS, group_size, row_count, HEAD_DIM), jnp.float32),
    )
    running = attend_block(running, own_block, own_start)
    stored = jnp.zeros((half_blocks, block_rows, 2 * kv_width), jnp.bfloat16)
    stored = lax.dynamic_update_index_in_dim(stored, own_block, 0, 0)

    def forward_turn(offset, carried):
        moving = passed_along(carried[1], "ctx", 1)
        kept = carried[2]
        return (attend_block(carried[0], moving, block_start(offset)), moving, kept)

    running, last_moving, stored = lax.fori_loop(
        1, half_blocks, forward_turn, (running, own_block, stored)
    )
    maxima, totals, summed = running
    attention = summed / totals[..., None]
    log_totals = maxima + jnp.log(totals)
    attention_low = (
        attention.transpose(2, 0, 1, 3).reshape(row_count, HEADS * HEAD_DIM).astype(jnp.bfloat16)
    )
    residual = inputs + jnp.dot(attention_low, out_full, preferred_element_type=jnp.float32)
    scale_two = rms_scale(residual)
    gain_second = gain_two.astype(jnp.float32)
    normed_two = (residual * scale_two * gain_second).astype(jnp.bfloat16)
    gate_pre = jnp.dot(normed_two, gate_full, preferred_element_type=jnp.float32)
    up_pre = jnp.dot(normed_two, up_full, preferred_element_type=jnp.float32)
    gate_sigmoid = jax.nn.sigmoid(gate_pre)
    gate_silu = gate_pre * gate_sigmoid
    hidden_low = (gate_silu * up_pre).astype(jnp.bfloat16)
    output = (residual + jnp.dot(hidden_low, down_full, preferred_element_type=jnp.float32)).astype(
        jnp.bfloat16
    )
    grad_down = jnp.einsum("rf,rd->fd", hidden_low, cotangent, preferred_element_type=jnp.float32)
    grad_hidden = jnp.einsum("rd,fd->rf", cotangent, down_full, preferred_element_type=jnp.float32)
    grad_gate_low = (
        grad_hidden * up_pre * (gate_sigmoid * (1.0 + gate_pre * (1.0 - gate_sigmoid)))
    ).astype(jnp.bfloat16)
    grad_up_low = (grad_hidden * gate_silu).astype(jnp.bfloat16)
    grad_gate = jnp.einsum(
        "rd,rf->df", normed_two, grad_gate_low, preferred_element_type=jnp.float32
    )
    grad_up = jnp.einsum("rd,rf->df", normed_two, grad_up_low, preferred_element_type=jnp.float32)
    grad_normed_two = jnp.einsum(
        "rf,df->rd", grad_gate_low, gate_full, preferred_element_type=jnp.float32
    ) + jnp.einsum("rf,df->rd", grad_up_low, up_full, preferred_element_type=jnp.float32)
    grad_from_second, grad_gain_two = norm_back(grad_normed_two, residual, scale_two, gain_second)
    grad_residual = cotangent.astype(jnp.float32) + grad_from_second
    grad_branch = grad_residual.astype(jnp.bfloat16)
    grad_out = jnp.einsum(
        "rd,re->de", attention_low, grad_branch, preferred_element_type=jnp.float32
    )
    grad_attention = jnp.einsum(
        "re,de->rd", grad_branch, out_full, preferred_element_type=jnp.float32
    ).astype(jnp.bfloat16)
    grad_grid = grad_attention.reshape(row_count, KV_HEADS, group_size, HEAD_DIM).transpose(
        1, 2, 0, 3
    )
    row_dots = jnp.sum(grad_grid.astype(jnp.float32) * attention, axis=-1)

    def gradient_block(query_grads, kv_block, key_start):
        current = query_grads
        masked, key_rows, value_rows = scores_of(kv_block, key_start)
        probability = jnp.exp(masked - log_totals[..., None])
        grad_values = jnp.einsum(
            "girk,gird->kgd",
            probability.astype(jnp.bfloat16),
            grad_grid,
            preferred_element_type=jnp.float32,
        )
        grad_probability = jnp.einsum(
            "gird,kgd->girk", grad_grid, value_rows, preferred_element_type=jnp.float32
        )
        grad_scores = (probability * (grad_probability - row_dots[..., None])).astype(jnp.bfloat16)
        current = (
            current
            + jnp.einsum(
                "girk,kgd->gird", grad_scores, key_rows, preferred_element_type=jnp.float32
            )
            * score_scale
        )
        grad_keys = (
            jnp.einsum(
                "girk,gird->kgd", grad_scores, query_grid, preferred_element_type=jnp.float32
            )
            * score_scale
        )
        return (
            current,
            jnp.concatenate(
                [
                    grad_keys.reshape(block_rows, kv_width),
                    grad_values.reshape(block_rows, kv_width),
                ],
                axis=1,
            ),
        )

    query_grads, partial_value = gradient_block(
        jnp.zeros((KV_HEADS, group_size, row_count, HEAD_DIM), jnp.float32), own_block, own_start
    )

    def backward_turn(offset, carried):
        query_grads, moving, moving_grads = carried
        moving = passed_along(moving, "ctx", 1)
        moving_grads = shifted(moving_grads.astype(jnp.bfloat16), "ctx", 1).astype(
            moving_grads.dtype
        )
        query_grads, partial_value = gradient_block(query_grads, moving, block_start(offset))
        return (query_grads, moving, moving_grads + partial_value)

    query_grads, moving, moving_grads = lax.fori_loop(
        1, half_blocks, backward_turn, (query_grads, own_block, partial_value)
    )
    home_grads = shifted(moving_grads.astype(jnp.bfloat16), "ctx", 1 - half_blocks).astype(
        moving_grads.dtype
    )
    own_grads = lax.psum_scatter(
        home_grads.astype(jnp.bfloat16), "wa", scatter_dimension=0, tiled=True
    ).astype(jnp.float32)
    grad_key_rot = own_grads[:, :kv_width].reshape(row_count, KV_HEADS, HEAD_DIM)
    grad_key_low = (
        unrotate(grad_key_rot, cosine_table, sine_table)
        .reshape(row_count, kv_width)
        .astype(jnp.bfloat16)
    )
    grad_value_low = own_grads[:, kv_width:].astype(jnp.bfloat16)
    grad_query_rot = query_grads.transpose(2, 0, 1, 3).reshape(row_count, HEADS, HEAD_DIM)
    grad_query_low = (
        unrotate(grad_query_rot, cosine_table, sine_table)
        .reshape(row_count, HEADS * HEAD_DIM)
        .astype(jnp.bfloat16)
    )
    grad_query_w = jnp.einsum(
        "rd,re->de", normed, grad_query_low, preferred_element_type=jnp.float32
    )
    grad_key_w = jnp.einsum("rd,re->de", normed, grad_key_low, preferred_element_type=jnp.float32)
    grad_value_w = jnp.einsum(
        "rd,re->de", normed, grad_value_low, preferred_element_type=jnp.float32
    )
    grad_normed = jnp.einsum(
        "re,de->rd", grad_query_low, query_full, preferred_element_type=jnp.float32
    )
    grad_normed = grad_normed + jnp.einsum(
        "re,de->rd", grad_key_low, key_full, preferred_element_type=jnp.float32
    )
    grad_normed = grad_normed + jnp.einsum(
        "re,de->rd", grad_value_low, value_full, preferred_element_type=jnp.float32
    )
    grad_from_first, grad_gain_one = norm_back(grad_normed, inputs, scale_one, gain_first)
    grad_tokens = (grad_residual + grad_from_first).astype(jnp.bfloat16)
    owned = (
        lax.psum_scatter(
            grad_query_w.astype(jnp.bfloat16), "wa", scatter_dimension=0, tiled=True
        ).astype(jnp.float32),
        lax.psum_scatter(
            grad_key_w.astype(jnp.bfloat16), "wa", scatter_dimension=0, tiled=True
        ).astype(jnp.float32),
        lax.psum_scatter(
            grad_value_w.astype(jnp.bfloat16), "wa", scatter_dimension=0, tiled=True
        ).astype(jnp.float32),
        lax.psum_scatter(
            grad_out.astype(jnp.bfloat16), "wa", scatter_dimension=0, tiled=True
        ).astype(jnp.float32),
        lax.psum_scatter(
            grad_gate.astype(jnp.bfloat16), "wa", scatter_dimension=0, tiled=True
        ).astype(jnp.float32),
        lax.psum_scatter(
            grad_up.astype(jnp.bfloat16), "wa", scatter_dimension=0, tiled=True
        ).astype(jnp.float32),
        lax.psum_scatter(
            grad_down.astype(jnp.bfloat16), "wa", scatter_dimension=0, tiled=True
        ).astype(jnp.float32),
        lax.psum_scatter(
            grad_gain_one.astype(jnp.bfloat16), "wa", scatter_dimension=0, tiled=True
        ).astype(jnp.float32),
        lax.psum_scatter(
            grad_gain_two.astype(jnp.bfloat16), "wa", scatter_dimension=0, tiled=True
        ).astype(jnp.float32),
    )
    totals_all = lax.psum(
        (owned[0], owned[1], owned[2], owned[3], owned[4], owned[5], owned[6], owned[7], owned[8]),
        "ctx",
    )
    return (
        output,
        grad_tokens,
        totals_all[0],
        totals_all[1],
        totals_all[2],
        totals_all[3],
        totals_all[4],
        totals_all[5],
        totals_all[6],
        totals_all[7],
        totals_all[8],
    )


def solution(mesh):
    return jax.shard_map(
        on_device,
        mesh=mesh,
        in_specs=(
            P(("ctx", "wa"), None),
            P(),
            P("wa", None),
            P("wa", None),
            P("wa", None),
            P("wa", None),
            P("wa", None),
            P("wa", None),
            P("wa", None),
            P("wa"),
            P("wa"),
            P(("ctx", "wa"), None),
        ),
        out_specs=(
            P(("ctx", "wa"), None),
            P(("ctx", "wa"), None),
            P("wa", None),
            P("wa", None),
            P("wa", None),
            P("wa", None),
            P("wa", None),
            P("wa", None),
            P("wa", None),
            P("wa"),
            P("wa"),
        ),
        check_vma=False,
    )
```

profile of v0, /device:TPU:0, one launch (start us, length us, event | category | flops | bytes accessed | tf_op | source)
XLA Modules:
  0.0 697.1 jit_solution(5693686064441868937)
XLA Ops:
  10.4 26.8 %while.68 = (s32[]{:T(128)}, u32[192]{0:T(256)S(1)}, u32[192]{0:T(256)S(1)}, s32[6144]{0:T(1024)}, s32[192]{0:T(256)S(1)}, /*index=5*/s32[]{:T(128)}, s32[]{:T(128)}, s32[]{}) while((s32[]{:T(128)}, u32[192]{0:T(256)S(1)}, u32[192]{0:T(256)S(1)}, s32[6144]{0:T(1024)}, s32[192]{0:T(256)S(1)}, /*index=5*/s32[]{:T(128)}, s32[]{:T(128)}, ...), condition=%wide.region_2.3_spmd.clone, body=%wide.region_1.2_spmd.clone.sunk | while | flops 4484 | bytes 17645 | solution.py:123
  38.9 8.5 %all-reduce.6 = (bf16[576]{0:T(1024)(128)(2,1)S(1)}, bf16[576]{0:T(1024)(128)(2,1)S(1)}) all-reduce(bf16[576]{0:T(1024)(128)(2,1)S(1)} %dynamic-update-slice, bf16[576]{0:T(1024)(128)(2,1)S(1)} %dynamic-update-slice.1), channel_id=1, replica_groups=mesh['ctx'=8,'wa'=4] {'wa'}, use_global_device_ids=true, to_apply=%add | all-reduce | flops 1152 | bytes 4608
  48.1 7.5 %all_gather.32 = bf16[576,192]{1,0:T(8,128)(2,1)S(1)} all-gather(bf16[144,192]{1,0:T(8,128)(2,1)S(1)} %copy-done.40), channel_id=1, replica_groups=mesh['ctx'=8,'wa'=4] {'wa'}, dimensions={0}, use_global_device_ids=true | all-gather | bytes 276480 | tf_op jit(solution)/shard_map/all_gather | solution.py:101
  63.7 10.2 %all_gather.34 = bf16[768,384]{1,0:T(8,128)(2,1)S(1)} all-gather(bf16[192,384]{1,0:T(8,128)(2,1)S(1)} %pad_maximum_fusion.2), channel_id=1, replica_groups=mesh['ctx'=8,'wa'=4] {'wa'}, dimensions={0}, use_global_device_ids=true | all-gather | bytes 737280 | tf_op jit(solution)/shard_map/all_gather | solution.py:141
  75.3 9.5 %all_gather.31 = bf16[576,576]{1,0:T(8,128)(2,1)S(1)} all-gather(bf16[144,576]{1,0:T(8,128)(2,1)S(1)} %copy-done.36), channel_id=1, replica_groups=mesh['ctx'=8,'wa'=4] {'wa'}, dimensions={0}, use_global_device_ids=true | all-gather | bytes 829440 | tf_op jit(solution)/shard_map/all_gather | solution.py:100
  97.0 62.3 %while.66 = (s32[]{:T(128)}, f32[3,3,192]{2,1,0:T(4,128)S(1)}, f32[3,3,192]{2,1,0:T(4,128)S(1)}, f32[3,3,192,64]{2,3,1,0:T(8,128)S(1)}, bf16[768,384]{0,1:T(8,12...) while((s32[]{:T(128)}, f32[3,3,192]{2,1,0:T(4,128)S(1)}, ...), condition=%wide.region_8.9_spmd.clone, body=%wide.region_5.8_spmd.clone.sunk | while | flops 355004736 | bytes 23058032 | solution.py:193
  101.0 12.7 %collective-permute-done = bf16[768,384]{0,1:T(8,128)(2,1)S(1)} collective-permute-done((bf16[768,384]{0,1:T(8,128)(2,1)S(1)}, bf16[768,384]{0,1:T(8,128)(2,1)S(1)}, u32[]{:S(2)}, u32[]{:S(2)}) %collective-permute-start) | collective-permute-done | bytes 589856 | tf_op jit(solution)/shard_map/while/body/eval_jaxpr/ppermute | solution.py:19
  122.8 11.9 %collective-permute-done = bf16[768,384]{0,1:T(8,128)(2,1)S(1)} collective-permute-done((bf16[768,384]{0,1:T(8,128)(2,1)S(1)}, bf16[768,384]{0,1:T(8,128)(2,1)S(1)}, u32[]{:S(2)}, u32[]{:S(2)}) %collective-permute-start) | collective-permute-done | bytes 589856 | tf_op jit(solution)/shard_map/while/body/eval_jaxpr/ppermute | solution.py:19
  143.9 11.0 %collective-permute-done = bf16[768,384]{0,1:T(8,128)(2,1)S(1)} collective-permute-done((bf16[768,384]{0,1:T(8,128)(2,1)S(1)}, bf16[768,384]{0,1:T(8,128)(2,1)S(1)}, u32[]{:S(2)}, u32[]{:S(2)}) %collective-permute-start) | collective-permute-done | bytes 589856 | tf_op jit(solution)/shard_map/while/body/eval_jaxpr/ppermute | solution.py:19
  159.4 7.9 %all_gather.35 = bf16[576,576]{1,0:T(8,128)(2,1)S(1)} all-gather(bf16[144,576]{1,0:T(8,128)(2,1)S(1)} %copy-done.37), channel_id=1, replica_groups=mesh['ctx'=8,'wa'=4] {'wa'}, dimensions={0}, use_global_device_ids=true | all-gather | bytes 829440 | tf_op jit(solution)/shard_map/all_gather | solution.py:103
  194.8 95.9 %while.67 = (s32[]{:T(128)}, f32[3,3,192,64]{2,3,1,0:T(8,128)S(1)}, bf16[768,384]{0,1:T(8,128)(2,1)}, bf16[768,384]{0,1:T(8,128)(2,1)}, s32[192]{0:T(256)S(1)}, ...) while((s32[]{:T(128)}, f32[3,3,192,64]{2,3,1,0:T(8,128)S(1)}, ...), condition=%wide.region_13.14_spmd.clone, body=%wide.region_12.13_spmd.clone.sunk | while | flops 864609216 | bytes 38607904 | solution.py:292
  204.3 10.2 %collective-permute-done.1 = bf16[768,384]{0,1:T(8,128)(2,1)S(1)} collective-permute-done((bf16[768,384]{0,1:T(8,128)(2,1)}, bf16[768,384]{0,1:T(8,128)(2,1)S(1)}, u32[]{:S(2)}, u32[]{:S(2)}) %collective-permute-start.1) | collective-permute-done | bytes 589856 | tf_op jit(solution)/shard_map/while/body/eval_jaxpr/ppermute | solution.py:19
  237.0 10.5 %collective-permute-done.1 = bf16[768,384]{0,1:T(8,128)(2,1)S(1)} collective-permute-done((bf16[768,384]{0,1:T(8,128)(2,1)}, bf16[768,384]{0,1:T(8,128)(2,1)S(1)}, u32[]{:S(2)}, u32[]{:S(2)}) %collective-permute-start.1) | collective-permute-done | bytes 589856 | tf_op jit(solution)/shard_map/while/body/eval_jaxpr/ppermute | solution.py:19
  269.0 10.5 %collective-permute-done.1 = bf16[768,384]{0,1:T(8,128)(2,1)S(1)} collective-permute-done((bf16[768,384]{0,1:T(8,128)(2,1)}, bf16[768,384]{0,1:T(8,128)(2,1)S(1)}, u32[]{:S(2)}, u32[]{:S(2)}) %collective-permute-start.1) | collective-permute-done | bytes 589856 | tf_op jit(solution)/shard_map/while/body/eval_jaxpr/ppermute | solution.py:19
  296.1 10.8 %collective-permute-done.3 = bf16[768,384]{0,1:T(8,128)(2,1)S(1)} collective-permute-done((bf16[768,384]{0,1:T(8,128)(2,1)}, bf16[768,384]{0,1:T(8,128)(2,1)S(1)}, u32[]{:S(2)}, u32[]{:S(2)}) %collective-permute-start.3) | collective-permute-done | bytes 589856 | tf_op jit(solution)/shard_map/ppermute | solution.py:25
  312.0 32.3 %reduce-scatter.25.cloned.1.call-done = bf16[192,384]{1,0:T(8,128)(2,1)} async-done(((bf16[768,384]{1,0:T(8,128)(2,1)}), bf16[192,384]{1,0:T(8,128)(2,1)}) %reduce-scatter.25.cloned.1.call-update) | async-done | bytes 147472
  363.5 6.9 reduce-scatter.19.cloned.1.call-done
  370.3 26.1 %reduce-scatter.13.cloned.1.call-done = bf16[144,576]{1,0:T(8,128)(2,1)} async-done(((bf16[576,576]{1,0:T(8,128)(2,1)}), bf16[144,576]{1,0:T(8,128)(2,1)}) %reduce-scatter.13.cloned.1.call-update) | async-done | bytes 165904 | tf_op jit(solution)/shard_map/reduce_scatter | solution.py:333
  406.3 13.5 %reduce-scatter.15.cloned.1.call-done = bf16[144,192]{1,0:T(8,128)(2,1)} async-done(((bf16[576,192]{1,0:T(8,128)(2,1)}), bf16[144,192]{1,0:T(8,128)(2,1)}) %reduce-scatter.15.cloned.1.call-update) | async-done | bytes 55312 | tf_op jit(solution)/shard_map/reduce_scatter | solution.py:336
  419.8 23.5 %reduce-scatter.17.cloned.1.call-done = bf16[144,192]{1,0:T(8,128)(2,1)} async-done(((bf16[576,192]{1,0:T(8,128)(2,1)}), bf16[144,192]{1,0:T(8,128)(2,1)}) %reduce-scatter.17.cloned.1.call-update) | async-done | bytes 55312 | tf_op jit(solution)/shard_map/reduce_scatter | solution.py:339
  443.3 33.2 %reduce-scatter.27.cloned.1.call-done = bf16[384,576]{1,0:T(8,128)(2,1)} async-done(((bf16[1536,576]{1,0:T(8,128)(2,1)}), bf16[384,576]{1,0:T(8,128)(2,1)}) %reduce-scatter.27.cloned.1.call-update) | async-done | bytes 442384
  477.8 30.8 %reduce-scatter.23.cloned.1.call-done = bf16[144,1536]{1,0:T(8,128)(2,1)} async-done(((bf16[576,1536]{1,0:T(8,128)(2,1)}), bf16[144,1536]{1,0:T(8,128)(2,1)}) %reduce-scatter.23.cloned.1.call-update) | async-done | bytes 442384 | tf_op jit(solution)/shard_map/reduce_scatter | solution.py:348
  508.6 32.0 %reduce-scatter.21.cloned.1.call-done = bf16[144,1536]{1,0:T(8,128)(2,1)} async-done(((bf16[576,1536]{1,0:T(8,128)(2,1)}), bf16[144,1536]{1,0:T(8,128)(2,1)}) %reduce-scatter.21.cloned.1.call-update) | async-done | bytes 442384 | tf_op jit(solution)/shard_map/reduce_scatter | solution.py:345
  540.6 150.0 %all-reduce.8 = (f32[144,576]{1,0:T(8,128)}, f32[144,192]{1,0:T(8,128)}, f32[144,192]{1,0:T(8,128)}, f32[144,576]{1,0:T(8,128)}, f32[144,1536]{1,0:T(8,128)}, /*...) all-reduce(bf16[144,576]{1,0:T(8,128)(2,1)S(1)} %copy-done.39, ...), channel_id=1, replica_groups=mesh['ctx'=8,'wa'=4] {'ctx'}, use_global_device_ids=true, to_apply=%region_17.18 | all-reduce | flops 885024 | bytes 5310720 | tf_op jit(solution)/shard_map/psum | solution.py:361
  (400 shorter events, 210.6 us)
Async XLA Ops:
  7.2 162.8 %all-gather.4.cloned.1.call-start = ((), (), s32[]{:S(2)}) async-start(), calls=%async_computation.8 | async-start | bytes 2211840 | tf_op jit(solution)/shard_map/all_gather | solution.py:104
  8.0 165.3 %all-gather.6.cloned.1.call-start = ((), (), s32[]{:S(2)}) async-start(), calls=%async_computation.9 | async-start | bytes 2211840 | tf_op jit(solution)/shard_map/all_gather | solution.py:105
  8.7 167.8 %all-gather.8.cloned.1.call-start = ((), (), s32[]{:S(2)}) async-start(), calls=%async_computation.10 | async-start | bytes 2211840 | tf_op jit(solution)/shard_map/all_gather | solution.py:106
  9.4 334.9 %reduce-scatter.25.cloned.1.call-start = ((), (), s32[]{:S(2)}) async-start(), calls=%async_computation.17 | async-start | bytes 737280
  55.9 254.5 %copy-start.28 = (f32[192,32]{0,1:T(8,128)}, f32[192,32]{0,1:T(8,128)S(1)}, u32[]{:S(2)}) copy-start(f32[192,32]{0,1:T(8,128)S(1)} %get-tuple-element.845) | copy-start | bytes 73732
  55.9 254.5 %copy-start.29 = (f32[192,32]{0,1:T(8,128)}, f32[192,32]{0,1:T(8,128)S(1)}, u32[]{:S(2)}) copy-start(f32[192,32]{0,1:T(8,128)S(1)} %get-tuple-element.846) | copy-start | bytes 73732
  97.0 16.7 %collective-permute-start = (bf16[768,384]{0,1:T(8,128)(2,1)S(1)}, bf16[768,384]{0,1:T(8,128)(2,1)S(1)}, u32[]{:S(2)}, u32[]{:S(2)}) collective-permute-start(bf16[768,384]{0,1:T(8,128)(2,1)S(1)} %get-tuple-element.1090), channel_id=1, source_target_pairs={{0,4},{4,8},{8,12},{12,16},{16,20},{20,24},{24,28},{1,5},{5,9},{9,... | collective-permute-start | bytes 1769480 | tf_op jit(solution)/shard_map/while/body/eval_jaxpr/ppermute | solution.py:19
  118.1 16.7 %collective-permute-start = (bf16[768,384]{0,1:T(8,128)(2,1)S(1)}, bf16[768,384]{0,1:T(8,128)(2,1)S(1)}, u32[]{:S(2)}, u32[]{:S(2)}) collective-permute-start(bf16[768,384]{0,1:T(8,128)(2,1)S(1)} %get-tuple-element.1090), channel_id=1, source_target_pairs={{0,4},{4,8},{8,12},{12,16},{16,20},{20,24},{24,28},{1,5},{5,9},{9,... | collective-permute-start | bytes 1769480 | tf_op jit(solution)/shard_map/while/body/eval_jaxpr/ppermute | solution.py:19
  139.2 15.8 %collective-permute-start = (bf16[768,384]{0,1:T(8,128)(2,1)S(1)}, bf16[768,384]{0,1:T(8,128)(2,1)S(1)}, u32[]{:S(2)}, u32[]{:S(2)}) collective-permute-start(bf16[768,384]{0,1:T(8,128)(2,1)S(1)} %get-tuple-element.1090), channel_id=1, source_target_pairs={{0,4},{4,8},{8,12},{12,16},{16,20},{20,24},{24,28},{1,5},{5,9},{9,... | collective-permute-start | bytes 1769480 | tf_op jit(solution)/shard_map/while/body/eval_jaxpr/ppermute | solution.py:19
  195.4 19.1 %collective-permute-start.1 = (bf16[768,384]{0,1:T(8,128)(2,1)}, bf16[768,384]{0,1:T(8,128)(2,1)S(1)}, u32[]{:S(2)}, u32[]{:S(2)}) collective-permute-start(bf16[768,384]{0,1:T(8,128)(2,1)} %get-tuple-element.1138), channel_id=1, source_target_pairs={{0,4},{4,8},{8,12},{12,16},{16,20},{20,24},{24,28},{1,5},{5,9},{9,... | collective-permute-start | bytes 1769480 | tf_op jit(solution)/shard_map/while/body/eval_jaxpr/ppermute | solution.py:19
  200.6 26.0 %collective-permute-start.2 = (bf16[768,384]{0,1:T(8,128)(2,1)}, bf16[768,384]{0,1:T(8,128)(2,1)S(1)}, u32[]{:S(2)}, u32[]{:S(2)}) collective-permute-start(bf16[768,384]{0,1:T(8,128)(2,1)} %get-tuple-element.1139), channel_id=1, source_target_pairs={{28,0},{0,4},{4,8},{8,12},{12,16},{16,20},{20,24},{24,28},{29,1},{... | collective-permute-start | bytes 1769480 | tf_op jit(solution)/shard_map/while/body/eval_jaxpr/ppermute | solution.py:25
  228.2 19.4 %collective-permute-start.1 = (bf16[768,384]{0,1:T(8,128)(2,1)}, bf16[768,384]{0,1:T(8,128)(2,1)S(1)}, u32[]{:S(2)}, u32[]{:S(2)}) collective-permute-start(bf16[768,384]{0,1:T(8,128)(2,1)} %get-tuple-element.1138), channel_id=1, source_target_pairs={{0,4},{4,8},{8,12},{12,16},{16,20},{20,24},{24,28},{1,5},{5,9},{9,... | collective-permute-start | bytes 1769480 | tf_op jit(solution)/shard_map/while/body/eval_jaxpr/ppermute | solution.py:19
  233.5 25.2 %collective-permute-start.2 = (bf16[768,384]{0,1:T(8,128)(2,1)}, bf16[768,384]{0,1:T(8,128)(2,1)S(1)}, u32[]{:S(2)}, u32[]{:S(2)}) collective-permute-start(bf16[768,384]{0,1:T(8,128)(2,1)} %get-tuple-element.1139), channel_id=1, source_target_pairs={{28,0},{0,4},{4,8},{8,12},{12,16},{16,20},{20,24},{24,28},{29,1},{... | collective-permute-start | bytes 1769480 | tf_op jit(solution)/shard_map/while/body/eval_jaxpr/ppermute | solution.py:25
  260.2 19.3 %collective-permute-start.1 = (bf16[768,384]{0,1:T(8,128)(2,1)}, bf16[768,384]{0,1:T(8,128)(2,1)S(1)}, u32[]{:S(2)}, u32[]{:S(2)}) collective-permute-start(bf16[768,384]{0,1:T(8,128)(2,1)} %get-tuple-element.1138), channel_id=1, source_target_pairs={{0,4},{4,8},{8,12},{12,16},{16,20},{20,24},{24,28},{1,5},{5,9},{9,... | collective-permute-start | bytes 1769480 | tf_op jit(solution)/shard_map/while/body/eval_jaxpr/ppermute | solution.py:19
  265.4 24.3 %collective-permute-start.2 = (bf16[768,384]{0,1:T(8,128)(2,1)}, bf16[768,384]{0,1:T(8,128)(2,1)S(1)}, u32[]{:S(2)}, u32[]{:S(2)}) collective-permute-start(bf16[768,384]{0,1:T(8,128)(2,1)} %get-tuple-element.1139), channel_id=1, source_target_pairs={{28,0},{0,4},{4,8},{8,12},{12,16},{16,20},{20,24},{24,28},{29,1},{... | collective-permute-start | bytes 1769480 | tf_op jit(solution)/shard_map/while/body/eval_jaxpr/ppermute | solution.py:25
  290.7 16.3 %collective-permute-start.3 = (bf16[768,384]{0,1:T(8,128)(2,1)}, bf16[768,384]{0,1:T(8,128)(2,1)S(1)}, u32[]{:S(2)}, u32[]{:S(2)}) collective-permute-start(bf16[768,384]{0,1:T(8,128)(2,1)} %get-tuple-element.1231), channel_id=1, source_target_pairs={{12,0},{16,4},{20,8},{24,12},{28,16},{0,20},{4,24},{8,28},{13,1},{... | collective-permute-start | bytes 1769480 | tf_op jit(solution)/shard_map/ppermute | solution.py:25
  308.1 62.3 %reduce-scatter.19.cloned.1.call-start = ((), (), s32[]{:S(2)}) async-start(), calls=%async_computation.14 | async-start | bytes 921600 | tf_op jit(solution)/shard_map/reduce_scatter | solution.py:342
  310.3 86.1 %reduce-scatter.13.cloned.1.call-start = ((), (), s32[]{:S(2)}) async-start(), calls=%async_computation.11 | async-start | bytes 921600 | tf_op jit(solution)/shard_map/reduce_scatter | solution.py:333
  312.0 107.9 %reduce-scatter.15.cloned.1.call-start = ((), (), s32[]{:S(2)}) async-start(), calls=%async_computation.12 | async-start | bytes 368640 | tf_op jit(solution)/shard_map/reduce_scatter | solution.py:336
  347.3 96.0 %reduce-scatter.17.cloned.1.call-start = ((), (), s32[]{:S(2)}) async-start(), calls=%async_computation.13 | async-start | bytes 368640 | tf_op jit(solution)/shard_map/reduce_scatter | solution.py:339
  349.4 127.2 %reduce-scatter.27.cloned.1.call-start = ((), (), s32[]{:S(2)}) async-start(), calls=%async_computation.18 | async-start | bytes 2457600
  353.6 155.0 %reduce-scatter.23.cloned.1.call-start = ((), (), s32[]{:S(2)}) async-start(), calls=%async_computation.16 | async-start | bytes 2211840 | tf_op jit(solution)/shard_map/reduce_scatter | solution.py:348
  356.7 183.9 %reduce-scatter.21.cloned.1.call-start = ((), (), s32[]{:S(2)}) async-start(), calls=%async_computation.15 | async-start | bytes 2211840 | tf_op jit(solution)/shard_map/reduce_scatter | solution.py:345
  398.1 142.5 %copy-start.38 = (bf16[144,576]{1,0:T(8,128)(2,1)S(1)}, bf16[144,576]{1,0:T(8,128)(2,1)}, u32[]{:S(2)}) copy-start(bf16[144,576]{1,0:T(8,128)(2,1)} %reduce-scatter.19.cloned.1.call-done) | copy-start | bytes 497668
  (61 other events, 897.2 us)
Sparse Core Ops, SparseCore 0:
  9.6 23.4 all-gather.3
  34.7 22.4 all-gather.5
  58.8 23.2 all-gather.7
  308.2 36.1 reduce-scatter.24
  347.3 22.9 reduce-scatter.18
  373.5 22.9 reduce-scatter.12
  399.5 20.2 reduce-scatter.14
  423.0 20.2 reduce-scatter.16
  445.9 30.6 reduce-scatter.26
  479.2 29.3 reduce-scatter.22
  511.2 29.3 reduce-scatter.20
where the time goes:
time: 699 us; the launch traced here: 697 us
  waiting for transfers between devices  287 us (41%)
  blocking collectives  205 us (29%)
  matrix products  80.6 us (12%)
  local copies, waits for them, and re-layouts  46.7 us (7%)
  starting transfers between devices  44.1 us (6%)
  other arithmetic  16.1 us (2%)
  between operations  16 us (2%)
    psum x1, blocking collectives, on_device(): lax.psum((owned[0], owned[1], owned[2], owned[3], owned[4], owned[5], own...  150 us
    unnamed x13, waiting for transfers between devices  67.7 us
    ppermute x6, waiting for transfers between devices, passed_along(): return lax.ppermute(shard, axis, pairs)  66.9 us
    reduce_scatter x1, waiting for transfers between devices, on_device(): lax.psum_scatter(grad_gate.astype(jnp.bfloat16), 'wa', scatter_dimension=...  32 us
    reduce_scatter x1, waiting for transfers between devices, on_device(): lax.psum_scatter(grad_up.astype(jnp.bfloat16), 'wa', scatter_dimension=0,...  30.8 us
    ppermute x6, starting transfers between devices, passed_along(): return lax.ppermute(shard, axis, pairs)  28.2 us
    reduce_scatter x1, waiting for transfers between devices, on_device(): lax.psum_scatter(grad_query_w.astype(jnp.bfloat16), 'wa', scatter_dimensi...  26.1 us
    gather x13, local copies, waits for them, and re-layouts, on_device(): jnp.searchsorted(segment_ids, query_segs, side='left')  25.8 us
  transfers between devices with their start and end apart: 21, of which 18 were waited for; matrix products, arithmetic and copies ran while one was open for 16% of the time, Pallas kernels for 0%

commit v1 on v0

--- a/solution.py
+++ b/solution.py
@@ -96,28 +96,26 @@
     kv_width = KV_HEADS * HEAD_DIM
     score_scale = HEAD_DIM ** (-0.5)
     row_start = (ctx_index * wa_count + wa_index) * row_count
-    gathered = (
-        lax.all_gather(w_query, "wa", axis=0, tiled=True),
-        lax.all_gather(w_key, "wa", axis=0, tiled=True),
-        lax.all_gather(w_value, "wa", axis=0, tiled=True),
-        lax.all_gather(w_out, "wa", axis=0, tiled=True),
-        lax.all_gather(w_gate, "wa", axis=0, tiled=True),
-        lax.all_gather(w_up, "wa", axis=0, tiled=True),
-        lax.all_gather(w_down, "wa", axis=0, tiled=True),
-        lax.all_gather(gain_attn, "wa", axis=0, tiled=True),
-        lax.all_gather(gain_ffn, "wa", axis=0, tiled=True),
-    )
-    (
-        query_full,
-        key_full,
-        value_full,
-        out_full,
-        gate_full,
-        up_full,
-        down_full,
-        gain_one,
-        gain_two,
-    ) = gathered
+    widths = tuple(
+        w.shape[1] for w in (w_query, w_key, w_value, w_out, w_gate, w_up)
+    )
+    early = jnp.concatenate(
+        [w_query, w_key, w_value, gain_attn[:, None], gain_ffn[:, None]], axis=1
+    )
+    early = lax.all_gather(early, "wa", axis=0, tiled=True)
+    late = lax.all_gather(
+        jnp.concatenate([w_out, w_gate, w_up], axis=1), "wa", axis=0, tiled=True
+    )
+    down_full = lax.all_gather(w_down, "wa", axis=0, tiled=True)
+    ends = (widths[0], widths[0] + widths[1], widths[0] + widths[1] + widths[2])
+    query_full = early[:, : ends[0]]
+    key_full = early[:, ends[0] : ends[1]]
+    value_full = early[:, ends[1] : ends[2]]
+    gain_one = early[:, ends[2]]
+    gain_two = early[:, ends[2] + 1]
+    out_full = late[:, : widths[3]]
+    gate_full = late[:, widths[3] : widths[3] + widths[4]]
+    up_full = late[:, widths[3] + widths[4] :]
     query_ids = row_start + jnp.arange(row_count, dtype=jnp.int32)
     query_segs = lax.dynamic_slice_in_dim(segment_ids, row_start, row_count)
     positions = query_ids - jnp.searchsorted(segment_ids, query_segs, side="left")
@@ -138,9 +136,51 @@
         rotate(key_pre, cosine_table, sine_table).astype(jnp.bfloat16).reshape(row_count, kv_width)
     )
     query_grid = query_low.reshape(row_count, KV_HEADS, group_size, HEAD_DIM).transpose(1, 2, 0, 3)
-    own_block = lax.all_gather(
-        jnp.concatenate([key_low, value_low], axis=1), "wa", axis=0, tiled=True
-    )
+    own_rows = jnp.concatenate([key_low, value_low], axis=1)
+    whole_half = half_blocks <= 4
+    if whole_half:
+        members = half_blocks * wa_count
+        halves = [list(range(members)), list(range(members, 2 * members))]
+        half_start = (ctx_index // half_blocks) * (half_blocks * block_rows)
+        half_rows = half_blocks * block_rows
+        half_kv = lax.all_gather(
+            own_rows, ("ctx", "wa"), axis=0, tiled=True, axis_index_groups=halves
+        )
+        half_keys = half_kv[:, :kv_width].reshape(half_rows, KV_HEADS, HEAD_DIM)
+        half_values = half_kv[:, kv_width:].reshape(half_rows, KV_HEADS, HEAD_DIM)
+        half_ids = half_start + jnp.arange(half_rows, dtype=jnp.int32)
+        half_segs = lax.dynamic_slice_in_dim(segment_ids, half_start, half_rows)
+        half_allowed = (query_segs[:, None] == half_segs[None, :]) & (
+            half_ids[None, :] <= query_ids[:, None]
+        )
+    else:
+        own_block = lax.all_gather(own_rows, "wa", axis=0, tiled=True)
+
+    def half_scores(group):
+        raw = (
+            jnp.einsum(
+                "ird,kd->irk",
+                query_grid[group],
+                half_keys[:, group],
+                preferred_element_type=jnp.float32,
+            )
+            * score_scale
+        )
+        return jnp.where(half_allowed[None], raw, MASKED_SCORE)
+
+    def half_forward(group):
+        masked = half_scores(group)
+        top = jnp.max(masked, axis=-1)
+        exponent = jnp.exp(masked - top[..., None])
+        total = jnp.sum(exponent, axis=-1)
+        summed = jnp.einsum(
+            "irk,kd->ird",
+            exponent.astype(jnp.bfloat16),
+            half_values[:, group],
+            preferred_element_type=jnp.float32,
+        )
+        return (top, total, summed)
+
     own_start = ctx_index * block_rows
 
     def block_start(offset):
@@ -175,24 +215,25 @@
         )
         return (new_max, totals, summed)
 
-    empty_max = jnp.full((KV_HEADS, group_size, row_count), MASKED_SCORE, jnp.float32)
-    running = (
-        empty_max,
-        jnp.zeros((KV_HEADS, group_size, row_count), jnp.float32),
-        jnp.zeros((KV_HEADS, group_size, row_count, HEAD_DIM), jnp.float32),
-    )
-    running = attend_block(running, own_block, own_start)
-    stored = jnp.zeros((half_blocks, block_rows, 2 * kv_width), jnp.bfloat16)
-    stored = lax.dynamic_update_index_in_dim(stored, own_block, 0, 0)
-
-    def forward_turn(offset, carried):
-        moving = passed_along(carried[1], "ctx", 1)
-        kept = carried[2]
-        return (attend_block(carried[0], moving, block_start(offset)), moving, kept)
-
-    running, last_moving, stored = lax.fori_loop(
-        1, half_blocks, forward_turn, (running, own_block, stored)
-    )
+    if whole_half:
+        parts = [half_forward(group) for group in range(KV_HEADS)]
+        running = tuple(jnp.stack(part) for part in zip(*parts))
+    else:
+        empty_max = jnp.full((KV_HEADS, group_size, row_count), MASKED_SCORE, jnp.float32)
+        running = (
+            empty_max,
+            jnp.zeros((KV_HEADS, group_size, row_count), jnp.float32),
+            jnp.zeros((KV_HEADS, group_size, row_count, HEAD_DIM), jnp.float32),
+        )
+        running = attend_block(running, own_block, own_start)
+
+        def forward_turn(offset, carried):
+            moving = passed_along(carried[1], "ctx", 1)
+            return (attend_block(carried[0], moving, block_start(offset)), moving)
+
+        running, last_moving = lax.fori_loop(
+            1, half_blocks, forward_turn, (running, own_block)
+        )
     maxima, totals, summed = running
     attention = summed / totals[..., None]
     log_totals = maxima + jnp.log(totals)
@@ -276,28 +317,71 @@
             ),
         )
 
-    query_grads, partial_value = gradient_block(
-        jnp.zeros((KV_HEADS, group_size, row_count, HEAD_DIM), jnp.float32), own_block, own_start
-    )
-
-    def backward_turn(offset, carried):
-        query_grads, moving, moving_grads = carried
-        moving = passed_along(moving, "ctx", 1)
-        moving_grads = shifted(moving_grads.astype(jnp.bfloat16), "ctx", 1).astype(
+    def half_backward(group):
+        masked = half_scores(group)
+        probability = jnp.exp(masked - log_totals[group][..., None])
+        grad_values = jnp.einsum(
+            "irk,ird->kd",
+            probability.astype(jnp.bfloat16),
+            grad_grid[group],
+            preferred_element_type=jnp.float32,
+        )
+        grad_probability = jnp.einsum(
+            "ird,kd->irk",
+            grad_grid[group],
+            half_values[:, group],
+            preferred_element_type=jnp.float32,
+        )
+        grad_scores = (probability * (grad_probability - row_dots[group][..., None])).astype(
+            jnp.bfloat16
+        )
+        query_part = (
+            jnp.einsum(
+                "irk,kd->ird", grad_scores, half_keys[:, group], preferred_element_type=jnp.float32
+            )
+            * score_scale
+        )
+        grad_keys = (
+            jnp.einsum(
+                "irk,ird->kd", grad_scores, query_grid[group], preferred_element_type=jnp.float32
+            )
+            * score_scale
+        )
+        return (query_part, grad_keys.astype(jnp.bfloat16), grad_values.astype(jnp.bfloat16))
+
+    if whole_half:
+        parts = [half_backward(group) for group in range(KV_HEADS)]
+        query_grads = jnp.stack([part[0] for part in parts])
+        own_grads = lax.psum_scatter(
+            jnp.concatenate([part[1] for part in parts] + [part[2] for part in parts], axis=1),
+            ("ctx", "wa"),
+            scatter_dimension=0,
+            tiled=True,
+            axis_index_groups=halves,
+        ).astype(jnp.float32)
+    else:
+        query_grads, partial_value = gradient_block(
+            jnp.zeros((KV_HEADS, group_size, row_count, HEAD_DIM), jnp.float32), own_block, own_start
+        )
+
+        def backward_turn(offset, carried):
+            query_grads, moving, moving_grads = carried
+            moving = passed_along(moving, "ctx", 1)
+            moving_grads = shifted(moving_grads.astype(jnp.bfloat16), "ctx", 1).astype(
+                moving_grads.dtype
+            )
+            query_grads, partial_value = gradient_block(query_grads, moving, block_start(offset))
+            return (query_grads, moving, moving_grads + partial_value)
+
+        query_grads, moving, moving_grads = lax.fori_loop(
+            1, half_blocks, backward_turn, (query_grads, own_block, partial_value)
+        )
+        home_grads = shifted(moving_grads.astype(jnp.bfloat16), "ctx", 1 - half_blocks).astype(
             moving_grads.dtype
         )
-        query_grads, partial_value = gradient_block(query_grads, moving, block_start(offset))
-        return (query_grads, moving, moving_grads + partial_value)
-
-    query_grads, moving, moving_grads = lax.fori_loop(
-        1, half_blocks, backward_turn, (query_grads, own_block, partial_value)
-    )
-    home_grads = shifted(moving_grads.astype(jnp.bfloat16), "ctx", 1 - half_blocks).astype(
-        moving_grads.dtype
-    )
-    own_grads = lax.psum_scatter(
-        home_grads.astype(jnp.bfloat16), "wa", scatter_dimension=0, tiled=True
-    ).astype(jnp.float32)
+        own_grads = lax.psum_scatter(
+            home_grads.astype(jnp.bfloat16), "wa", scatter_dimension=0, tiled=True
+        ).astype(jnp.float32)
     grad_key_rot = own_grads[:, :kv_width].reshape(row_count, KV_HEADS, HEAD_DIM)
     grad_key_low = (
         unrotate(grad_key_rot, cosine_table, sine_table)
@@ -329,51 +413,29 @@
     )
     grad_from_first, grad_gain_one = norm_back(grad_normed, inputs, scale_one, gain_first)
     grad_tokens = (grad_residual + grad_from_first).astype(jnp.bfloat16)
-    owned = (
-        lax.psum_scatter(
-            grad_query_w.astype(jnp.bfloat16), "wa", scatter_dimension=0, tiled=True
-        ).astype(jnp.float32),
-        lax.psum_scatter(
-            grad_key_w.astype(jnp.bfloat16), "wa", scatter_dimension=0, tiled=True
-        ).astype(jnp.float32),
-        lax.psum_scatter(
-            grad_value_w.astype(jnp.bfloat16), "wa", scatter_dimension=0, tiled=True
-        ).astype(jnp.float32),
-        lax.psum_scatter(
-            grad_out.astype(jnp.bfloat16), "wa", scatter_dimension=0, tiled=True
-        ).astype(jnp.float32),
-        lax.psum_scatter(
-            grad_gate.astype(jnp.bfloat16), "wa", scatter_dimension=0, tiled=True
-        ).astype(jnp.float32),
-        lax.psum_scatter(
-            grad_up.astype(jnp.bfloat16), "wa", scatter_dimension=0, tiled=True
-        ).astype(jnp.float32),
-        lax.psum_scatter(
-            grad_down.astype(jnp.bfloat16), "wa", scatter_dimension=0, tiled=True
-        ).astype(jnp.float32),
-        lax.psum_scatter(
-            grad_gain_one.astype(jnp.bfloat16), "wa", scatter_dimension=0, tiled=True
-        ).astype(jnp.float32),
-        lax.psum_scatter(
-            grad_gain_two.astype(jnp.bfloat16), "wa", scatter_dimension=0, tiled=True
-        ).astype(jnp.float32),
-    )
-    totals_all = lax.psum(
-        (owned[0], owned[1], owned[2], owned[3], owned[4], owned[5], owned[6], owned[7], owned[8]),
-        "ctx",
+
+    def summed_grads(parts):
+        joined = jnp.concatenate([part.astype(jnp.bfloat16) for part in parts], axis=1)
+        owned = lax.psum_scatter(joined, "wa", scatter_dimension=0, tiled=True)
+        return lax.psum(owned, "ctx").astype(jnp.float32)
+
+    total_down = summed_grads([grad_down])
+    total_late = summed_grads([grad_out, grad_gate, grad_up])
+    total_early = summed_grads(
+        [grad_query_w, grad_key_w, grad_value_w, grad_gain_one[:, None], grad_gain_two[:, None]]
     )
     return (
         output,
         grad_tokens,
-        totals_all[0],
-        totals_all[1],
-        totals_all[2],
-        totals_all[3],
-        totals_all[4],
-        totals_all[5],
-        totals_all[6],
-        totals_all[7],
-        totals_all[8],
+        total_early[:, : ends[0]],
+        total_early[:, ends[0] : ends[1]],
+        total_early[:, ends[1] : ends[2]],
+        total_late[:, : widths[3]],
+        total_late[:, widths[3] : widths[3] + widths[4]],
+        total_late[:, widths[3] + widths[4] :],
+        total_down,
+        total_early[:, ends[2]],
+        total_early[:, ends[2] + 1],
     )
 
 

time: 699 us -> 449 us (0.64)
  blocking collectives: 205 us -> 0 us
  starting transfers between devices: 44.1 us -> 0.37 us
  local copies, waits for them, and re-layouts: 46.7 us -> 75.9 us
  waiting for transfers between devices: 287 us -> 270 us
  matrix products: 80.6 us -> 68.5 us
    psum x1 -> x0, blocking collectives: 150 us -> none  [on_device(): lax.psum((owned[0], owned[1], owned[2], owned[3], owned[4], owned[5], own...]
    psum x0 -> x1, waiting for transfers between devices: none -> 97.2 us  [summed_grads(): return lax.psum(owned, 'ctx').astype(jnp.float32)]
    ppermute x10 -> x0, waiting for transfers between devices: 86.8 us -> none  [the longest x6 66.9 us: passed_along(): return lax.ppermute(shard, axis, pairs)]
    reduce_scatter x6 -> x2, waiting for transfers between devices: 133 us -> 74.1 us  [summed_grads(): owned = lax.psum_scatter(joined, 'wa', scatter_dimension=0, tiled=True)]
    all_gather x3 -> x4, waiting for transfers between devices: 0.02 us -> 47.1 us  [the longest x1 30.9 us: on_device(): lax.all_gather(own_rows, ('ctx', 'wa'), axis=0, tiled=True, axis_index_gr...]
    ppermute x10 -> x0, starting transfers between devices: 43.7 us -> none  [the longest x6 28.2 us: passed_along(): return lax.ppermute(shard, axis, pairs)]
    all_gather x5 -> x0, blocking collectives: 41.1 us -> none  [the longest x1 10.2 us: on_device(): lax.all_gather(jnp.concatenate([key_low, value_low], axis=1), 'wa', axis=...]
    unnamed x13 -> x11, waiting for transfers between devices: 67.7 us -> 51.5 us
  transfers between devices with their start and end apart: 21 -> 9, of which waited for: 18 -> 8; matrix products, arithmetic and copies ran while one was open for 16% -> 24% of each run, Pallas kernels for 0% -> 0%
where the time goes in v1:
time: 449 us; the launch traced here: 443 us
  waiting for transfers between devices  270 us (60%)
  local copies, waits for them, and re-layouts  75.9 us (17%)
  matrix products  68.5 us (15%)
  between operations  15.3 us (3%)
  other arithmetic  12.6 us (3%)
    psum x1, waiting for transfers between devices, summed_grads(): return lax.psum(owned, 'ctx').astype(jnp.float32)  97.2 us
    reduce_scatter x2, waiting for transfers between devices, summed_grads(): owned = lax.psum_scatter(joined, 'wa', scatter_dimension=0, tiled=True)  74.1 us
    unnamed x11, waiting for transfers between devices  51.5 us
    all_gather x1, waiting for transfers between devices, on_device(): lax.all_gather(own_rows, ('ctx', 'wa'), axis=0, tiled=True, axis_index_gr...  30.9 us
    gather x13, local copies, waits for them, and re-layouts, on_device(): jnp.searchsorted(segment_ids, query_segs, side='left')  25.8 us
    unnamed x120, local copies, waits for them, and re-layouts  13.8 us
    all_gather x1, waiting for transfers between devices, on_device(): lax.all_gather(jnp.concatenate([w_out, w_gate, w_up], axis=1), 'wa', axis...  13 us
    concatenate x2, local copies, waits for them, and re-layouts, summed_grads(): jnp.concatenate([part.astype(jnp.bfloat16) for part in parts], axis=1)  11.4 us
  transfers between devices with their start and end apart: 9, of which 8 were waited for; matrix products, arithmetic and copies ran while one was open for 24% of the time, Pallas kernels for 0%

profile of v1, /device:TPU:0, one launch (start us, length us, event | category | flops | bytes accessed | tf_op | source)
XLA Modules:
  0.0 443.1 jit_solution(9773610378974921672)
XLA Ops:
  12.3 26.8 %while.24 = (s32[]{:T(128)}, u32[192]{0:T(256)S(1)}, u32[192]{0:T(256)S(1)}, s32[6144]{0:T(1024)}, s32[192]{0:T(256)S(1)}, /*index=5*/s32[]{:T(128)}, s32[]{:T(128)}, s32[]{}) while((s32[]{:T(128)}, u32[192]{0:T(256)S(1)}, u32[192]{0:T(256)S(1)}, s32[6144]{0:T(1024)}, s32[192]{0:T(256)S(1)}, /*index=5*/s32[]{:T(128)}, s32[]{:T(128)}, ...), condition=%wide.region_2.3_spmd.clone, body=%wide.region_1.2_spmd.clone.sunk | while | flops 4484 | bytes 17645 | solution.py:121
  50.2 3.1 all-gather.11.cloned.1.call-done
  53.3 3.1 fusion.130
  56.4 30.9 %all-gather.7.cloned.1.call-done = bf16[3072,384]{1,0:T(8,128)(2,1)} async-done(((bf16[192,384]{1,0:T(8,128)(2,1)}), bf16[3072,384]{1,0:T(8,128)(2,1)}) %all-gather.7.cloned.1.call-update) | async-done | bytes 2359312 | tf_op jit(solution)/shard_map/all_gather | solution.py:146
  87.4 3.8 fusion.124
  94.5 2.9 fusion.127
  109.8 13.0 %all-gather.9.cloned.1.call-done = bf16[576,3648]{1,0:T(8,128)(2,1)} async-done(((bf16[144,3648]{1,0:T(8,128)(2,1)}), bf16[576,3648]{1,0:T(8,128)(2,1)}) %all-gather.9.cloned.1.call-update) | async-done | bytes 4202512 | tf_op jit(solution)/shard_map/all_gather | solution.py:106
  124.8 2.5 fusion.67
  127.3 2.3 multiply_convert_fusion.4
  134.4 5.2 %multiply_convert_fusion.2 = bf16[3,192,3072]{2,1,0:T(8,128)(2,1)S(1)} fusion(f32[3,192,3072]{2,1,0:T(8,128)} %copy-done.3, f32[3,192]{1,0:T(4,128)S(1)} %get-tuple-element.140, f32[3,192]{1,0:T(4,128)S(1)} %get-tuple-element.137, bf16[3072,3,64]{0,2,1:T(8,128)(2,1)} %bitcast.197, bf16[3,3,192,64]{2,3,1,0:T(8,128)(2,1)} %bitcast.201), kind=kOutput, calls=%fused_computation.11 | convolution fusion | flops 233570304 | bytes 11112960 | tf_op jit(solution)/shard_map/ird,kd->irk/dot_general | solution.py:329
  152.4 2.3 fusion.50
  154.8 4.3 copy.73
  159.2 3.1 convolution_convert_fusion
  162.3 3.9 copy.75
  167.1 3.8 fusion.81
  174.2 44.4 %reduce-scatter.13.cloned.1.call-done = bf16[192,384]{1,0:T(8,128)(2,1)} async-done(((bf16[3072,384]{1,0:T(8,128)(2,1)}), bf16[192,384]{1,0:T(8,128)(2,1)}) %reduce-scatter.13.cloned.1.call-update) | async-done | bytes 147472
  225.9 3.3 concatenate.49
  232.2 3.0 convolution_convert_fusion.1
  235.3 8.2 %concatenate.50 = bf16[576,3648]{1,0:T(8,128)(2,1)} concatenate(bf16[576,576]{1,0:T(8,128)(2,1)} %convolution_convert_fusion.3, bf16[576,1536]{1,0:T(8,128)(2,1)S(1)} %convolution_convert_fusion.2, bf16[576,1536]{1,0:T(8,128)(2,1)} %convolution_convert_fusion.1), dimensions={1} | concatenate | bytes 8404992 | tf_op jit(solution)/shard_map/concatenate | solution.py:418
  243.5 6.3 %reduce-scatter.15.cloned.1.call-done = bf16[384,576]{1,0:T(8,128)(2,1)} async-done(((bf16[1536,576]{1,0:T(8,128)(2,1)}), bf16[384,576]{1,0:T(8,128)(2,1)}) %reduce-scatter.15.cloned.1.call-update) | async-done | bytes 442384
  251.8 26.5 %reduce-scatter.9.cloned.1.call-done = bf16[144,962]{1,0:T(8,128)(2,1)} async-done(((bf16[576,962]{1,0:T(8,128)(2,1)}), bf16[144,962]{1,0:T(8,128)(2,1)}) %reduce-scatter.9.cloned.1.call-update) | async-done | bytes 277072 | tf_op jit(solution)/shard_map/reduce_scatter | solution.py:419
  278.3 47.6 %reduce-scatter.11.cloned.1.call-done = bf16[144,3648]{1,0:T(8,128)(2,1)} async-done(((bf16[576,3648]{1,0:T(8,128)(2,1)}), bf16[144,3648]{1,0:T(8,128)(2,1)}) %reduce-scatter.11.cloned.1.call-update) | async-done | bytes 1050640 | tf_op jit(solution)/shard_map/reduce_scatter | solution.py:419
  326.0 2.6 fusion.77
  329.4 97.2 %all-reduce.3.cloned.1.call-done = (bf16[144,962]{1,0:T(8,128)(2,1)}, bf16[144,3648]{1,0:T(8,128)(2,1)}, bf16[384,576]{0,1:T(8,128)(2,1)}) async-done(((bf16[144,962]{1,0:T(8,128)(2,1)}, bf16[144,3648]{1,0:T(8,128)(2,1)}, bf16[384,576]{0,1:T(8,128)(2,1)}), (bf16[144,962]{1,0:T(8,128)(2,1)}, bf16[144,3648]{1,0:T(8,128)(2,1)}, bf16[384,576]{0,1:T(8,128)(2,1)})) %all-reduce.3.cloned.1.call-update) | async-done | bytes 1770064 | tf_op jit(solution)/shard_map/psum | solution.py:420
  (304 shorter events, 104.0 us)
Async XLA Ops:
  7.2 32.9 %all-gather.5.cloned.1.call-start = ((), (), s32[]{:S(2)}) async-start(), calls=%async_computation.4 | async-start | bytes 1474560 | tf_op jit(solution)/shard_map/all_gather | solution.py:105
  8.7 30.4 %copy-start.21 = (bf16[192,576]{1,0:T(8,128)(2,1)S(1)}, bf16[192,576]{1,0:T(8,128)(2,1)}, u32[]{:S(2)}) copy-start(bf16[192,576]{1,0:T(8,128)(2,1)} %param.14) | copy-start | bytes 663556
  10.7 42.6 %all-gather.11.cloned.1.call-start = ((), (), s32[]{:S(2)}) async-start(), calls=%async_computation.7 | async-start | bytes 2211840 | tf_op jit(solution)/shard_map/all_gather | solution.py:109
  11.4 76.0 %all-gather.7.cloned.1.call-start = ((), (), s32[]{:S(2)}) async-start(), calls=%async_computation.5 | async-start | bytes 2506752 | tf_op jit(solution)/shard_map/all_gather | solution.py:146
  12.3 33.6 %copy-start.43 = (bf16[144,1536]{1,0:T(8,128)(2,1)S(1)}, bf16[144,1536]{1,0:T(8,128)(2,1)}, u32[]{:S(2)}) copy-start(bf16[144,1536]{1,0:T(8,128)(2,1)} %param.20) | copy-start | bytes 1327108
  12.3 33.6 %copy-start.44 = (bf16[144,1536]{1,0:T(8,128)(2,1)S(1)}, bf16[144,1536]{1,0:T(8,128)(2,1)}, u32[]{:S(2)}) copy-start(bf16[144,1536]{1,0:T(8,128)(2,1)} %param.21) | copy-start | bytes 1327108
  12.3 33.6 %copy-start.46 = (bf16[144,576]{1,0:T(8,128)(2,1)S(1)}, bf16[144,576]{1,0:T(8,128)(2,1)}, u32[]{:S(2)}) copy-start(bf16[144,576]{1,0:T(8,128)(2,1)} %param.19) | copy-start | bytes 497668
  45.8 77.1 %all-gather.9.cloned.1.call-start = ((), (), s32[]{:S(2)}) async-start(), calls=%async_computation.6 | async-start | bytes 5345280 | tf_op jit(solution)/shard_map/all_gather | solution.py:106
  48.0 170.5 %reduce-scatter.13.cloned.1.call-start = ((), (), s32[]{:S(2)}) async-start(), calls=%async_computation.10 | async-start | bytes 2506752
  50.2 52.7 %copy-start.27 = (bf16[3,3,192,64]{2,3,1,0:T(8,128)(2,1)}, bf16[3,3,192,64]{2,3,1,0:T(8,128)(2,1)S(1)}, u32[]{:S(2)}) copy-start(bf16[3,3,192,64]{2,3,1,0:T(8,128)(2,1)S(1)} %maximum_bitcast_fusion) | copy-start | bytes 663556
  92.8 15.5 %copy-start.7 = (bf16[3072,192]{0,1:T(8,128)(2,1)}, bf16[3072,192]{0,1:T(8,128)(2,1)S(1)}, u32[]{:S(2)}) copy-start(bf16[3072,192]{0,1:T(8,128)(2,1)S(1)} %copy.66) | copy-start | bytes 3538948
  108.4 16.3 %copy-start.47 = (f32[576]{0:T(1024)S(1)}, f32[576]{0:T(1024)}, u32[]{:S(2)}) copy-start(f32[576]{0:T(1024)} %get-tuple-element.95) | copy-start | bytes 6916
  109.8 17.5 %copy-start.30 = (f32[192,1536]{1,0:T(8,128)S(1)}, f32[192,1536]{1,0:T(8,128)}, u32[]{:S(2)}) copy-start(f32[192,1536]{1,0:T(8,128)} %fusion.130) | copy-start | bytes 3538948
  159.1 90.7 %reduce-scatter.15.cloned.1.call-start = ((), (), s32[]{:S(2)}) async-start(), calls=%async_computation.11 | async-start | bytes 2457600
  166.2 112.1 %reduce-scatter.9.cloned.1.call-start = ((), (), s32[]{:S(2)}) async-start(), calls=%async_computation.8 | async-start | bytes 1474560 | tf_op jit(solution)/shard_map/reduce_scatter | solution.py:419
  173.4 46.3 %copy-start.35 = (f32[192,32]{0,1:T(8,128)S(1)}, f32[192,32]{0,1:T(8,128)}, u32[]{:S(2)}) copy-start(f32[192,32]{0,1:T(8,128)} %copy-done.33) | copy-start | bytes 73732
  173.4 46.3 %copy-start.38 = (f32[192,32]{0,1:T(8,128)S(1)}, f32[192,32]{0,1:T(8,128)}, u32[]{:S(2)}) copy-start(f32[192,32]{0,1:T(8,128)} %copy-done.36) | copy-start | bytes 73732
  173.4 46.4 %copy-start.23 = (bf16[192,576]{1,0:T(8,128)(2,1)S(1)}, bf16[192,576]{1,0:T(8,128)(2,1)}, u32[]{:S(2)}) copy-start(bf16[192,576]{1,0:T(8,128)(2,1)} %param.14) | copy-start | bytes 663556
  173.4 49.6 %copy-start.25 = (bf16[576,962]{1,0:T(8,128)(2,1)S(1)}, bf16[576,962]{1,0:T(8,128)(2,1)}, u32[]{:S(2)}) copy-start(bf16[576,962]{1,0:T(8,128)(2,1)} %all-gather.5.cloned.1.call-done) | copy-start | bytes 3324676
  229.2 96.8 %reduce-scatter.11.cloned.1.call-start = ((), (), s32[]{:S(2)}) async-start(), calls=%async_computation.9 | async-start | bytes 5345280 | tf_op jit(solution)/shard_map/reduce_scatter | solution.py:419
  243.4 82.5 %copy-start.11 = (bf16[1536,576]{0,1:T(8,128)(2,1)S(1)}, bf16[1536,576]{0,1:T(8,128)(2,1)}, u32[]{:S(2)}) copy-start(bf16[1536,576]{0,1:T(8,128)(2,1)} %all-gather.11.cloned.1.call-done) | copy-start | bytes 5308420
  243.4 82.6 %copy-start.17 = (f32[192,576]{1,0:T(8,128)S(1)}, f32[192,576]{1,0:T(8,128)}, u32[]{:S(2)}) copy-start(f32[192,576]{1,0:T(8,128)} %copy-done.16) | copy-start | bytes 1327108
  243.4 85.1 %copy-start.50 = (f32[192]{0:T(256)S(1)}, f32[192]{0:T(256)}, u32[]{:S(2)}) copy-start(f32[192]{0:T(256)} %get-tuple-element.145) | copy-start | bytes 2308
  243.5 183.1 %all-reduce.3.cloned.1.call-start = ((), (), s32[]{:S(2)}) async-start(), calls=%async_computation.12 | async-start | bytes 3612672 | tf_op jit(solution)/shard_map/psum | solution.py:420
  (43 other events, 226.9 us)
Sparse Core Ops, SparseCore 0:
  10.8 20.1 all-gather.4
  32.5 20.7 all-gather.10
  55.5 31.8 all-gather.6
  88.8 34.0 all-gather.8
  159.2 59.2 reduce-scatter.12
  221.0 28.8 reduce-scatter.14
  252.6 25.6 reduce-scatter.8
  280.8 45.0 reduce-scatter.10
  330.9 95.6 all-reduce.2
